TPU v7x, 32 devices: a whole 2x2x4 slice. The times are simulated.
32 devices in a mesh: row: 4 (over x, core), col: 2 (over y), layer: 4 (over z).
Axes of the slice: x: 2, y: 2, z: 4, core: 2. Of those that a mesh axis runs over, the one named last changes fastest.
Arguments:
- matrix_values: float32 [4, 1024, 4, 1024], P(None, 'row', 'layer', 'col'), may hold values from 4.8828125e-08 to 1.2001953
- matrix_pattern: int32 [4, 4, 4, 4], P(None, 'row', 'layer', 'col'), may hold values from 0 to 1, as said below
- panel: float32 [4, 1024, 1024], P('layer', 'row', 'col'), may hold values from 0.0009 to 1097
- panel_pattern: int32 [4, 4, 4], P('layer', 'row', 'col'), may hold values from 0 to 1, as said below
- out_pattern: int32 [4, 4, 4], P('layer', 'row', 'col'), may hold values from 0 to 1, as said below
Outputs:
- inflated: float32 [4, 1024, 1024], P('layer', 'row', 'col')
Inputs may be any that keep to these rules, and one draw needn't show every extreme that they name: `matrix_pattern`: every tile on the diagonal of the 4096 x 4096 matrix is present. `panel_pattern`: for every column tile, some row tile is present both here and in out_pattern. `out_pattern`: for every column tile, some row tile is present both here and in panel_pattern.
All inputs are finite; a program needn't handle non-finite values.
Results may differ from a plain program's by a relative error of at most 0.0001.
Values sent between devices are 32-bit elements; how exact they have to be, the bound alone decides.
A program may use at most 64 MiB of HBM per device.

v0:
```python
import jax
import jax.numpy as jnp
from jax import lax
from jax.sharding import PartitionSpec as P

TILE = 256
PRODUCTS = 2


def spread(pattern, dimensions):
    grown = pattern.astype(jnp.float32)
    for dimension in dimensions:
        grown = jnp.repeat(grown, TILE, axis=dimension)
    return grown


def body(matrix_values, matrix_pattern, panel, panel_pattern, out_pattern):
    live_matrix = matrix_values * spread(matrix_pattern, (1, 3))
    current = panel * spread(panel_pattern, (1, 2))
    for stepnum in range(PRODUCTS):
        panel_part = lax.all_gather(current, "row", axis=1, tiled=True)[0]
        partial_value = jnp.einsum(
            "abk,kc->abc",
            lax.all_gather(live_matrix, "col", axis=3, tiled=True)[:, :, 0, :],
            panel_part,
            precision=lax.Precision.HIGHEST,
            preferred_element_type=jnp.float32,
        )
        current = lax.psum_scatter(partial_value, "layer", scatter_dimension=0, tiled=True)
    kept_cells = spread(out_pattern, (1, 2))[0]
    squared = current[0] * current[0] * kept_cells
    local_total = jnp.sum(squared, axis=0)
    local_kept = jnp.sum(kept_cells, axis=0)
    column_total, kept = lax.psum((local_total, local_kept), ("row", "layer"))
    inflated = squared * (kept / column_total)[None, :]
    return inflated[None, :, :]


def solution(mesh):
    placed = (
        P(None, "row", "layer", "col"),
        P(None, "row", "layer", "col"),
        P("layer", "row", "col"),
        P("layer", "row", "col"),
        P("layer", "row", "col"),
    )
    return jax.shard_map(
        body, mesh=mesh, in_specs=placed, out_specs=P("layer", "row", "col"), check_vma=False
    )
```

profile of v0, /device:TPU:0, one launch (start us, length us, event | category | flops | bytes accessed | tf_op | source)
XLA Modules:
  0.0 266.9 jit_solution(6729607009257796455)
XLA Ops:
  6.5 0.0 all-gather.6.cloned.1.call-start
  6.5 0.7 convert_bitcast_fusion.2
  7.2 0.1 broadcast_bitcast_fusion.2
  7.3 1.9 broadcast_multiply_fusion
  9.2 0.0 all-gather.6.cloned.1.call-update
  9.2 0.0 all-gather.4.cloned.1.call-start
  9.2 0.7 convert_bitcast_fusion
  9.9 0.1 copy.6
  10.0 0.1 broadcast_bitcast_fusion
  10.1 3.2 %copy_multiply_fusion = f32[4,256,1,512]{3,1,0,2:T(8,128)} fusion(f32[4,256,1,512]{3,2,1,0:T(1,128)} %param.5, f32[4,512]{1,0:T(4,128)S(1)} %bitcast.28), kind=kLoop, calls=%fused_computation.6 | loop fusion | flops 524288 | bytes 4202496 | tf_op jit(solution)/shard_map/mul | solution.py:18
  13.3 0.0 all-gather.4.cloned.1.call-update
  13.4 0.0 reduce-scatter.3.cloned.1.call-start
  13.4 21.3 %all-gather.6.cloned.1.call-done = f32[1,1024,512]{2,1,0:T(8,128)} async-done(((f32[1,256,512]{2,1,0:T(8,128)}), f32[1,1024,512]{2,1,0:T(8,128)}) %all-gather.6.cloned.1.call-update) | async-done | bytes 2097168 | tf_op jit(solution)/shard_map/all_gather | solution.py:21
  34.7 58.3 %all-gather.4.cloned.1.call-done = f32[4,256,1,1024]{3,1,0,2:T(8,128)} async-done(((f32[4,256,1,512]{3,1,0,2:T(8,128)}), f32[4,256,1,1024]{3,1,0,2:T(8,128)}) %all-gather.4.cloned.1.call-update) | async-done | bytes 4194320 | tf_op jit(solution)/shard_map/all_gather | solution.py:24
  93.0 10.5 %fusion.2 = f32[4,256,512]{2,1,0:T(8,128)} fusion(f32[4,256,1,1024]{3,1,0,2:T(8,128)} %all-gather.4.cloned.1.call-done, f32[1,1024,512]{2,1,0:T(8,128)} %all-gather.6.cloned.1.call-done), kind=kOutput, calls=%fused_computation.2 | convolution fusion | flops 6442450944 | bytes 8388608 | tf_op jit(solution)/shard_map/abk,kc->abc/dot_general | solution.py:22
  103.5 0.0 reduce-scatter.3.cloned.1.call-update
  103.5 0.0 all-gather.8.cloned.1.call-start
  103.6 44.0 %reduce-scatter.3.cloned.1.call-done = f32[1,256,512]{2,1,0:T(8,128)} async-done(((f32[4,256,512]{2,1,0:T(8,128)}), f32[1,256,512]{2,1,0:T(8,128)}) %reduce-scatter.3.cloned.1.call-update) | async-done | bytes 524304 | tf_op jit(solution)/shard_map/reduce_scatter | solution.py:29
  147.5 0.0 all-gather.8.cloned.1.call-update
  147.6 0.0 reduce-scatter.5.cloned.1.call-start
  147.6 23.4 %all-gather.8.cloned.1.call-done = f32[1,1024,512]{2,1,0:T(8,128)} async-done(((f32[1,256,512]{2,1,0:T(8,128)}), f32[1,1024,512]{2,1,0:T(8,128)}) %all-gather.8.cloned.1.call-update) | async-done | bytes 2097168 | tf_op jit(solution)/shard_map/all_gather | solution.py:21
  171.0 10.5 %fusion = f32[4,256,512]{2,1,0:T(8,128)} fusion(f32[4,256,1,1024]{3,1,0,2:T(8,128)} %all-gather.4.cloned.1.call-done, f32[1,1024,512]{2,1,0:T(8,128)} %all-gather.8.cloned.1.call-done), kind=kOutput, calls=%fused_computation | convolution fusion | flops 6442450944 | bytes 8388608 | tf_op jit(solution)/shard_map/abk,kc->abc/dot_general | solution.py:22
  181.5 0.0 copy-start
  181.5 0.0 reduce-scatter.5.cloned.1.call-update
  181.5 0.6 copy-done
  182.1 0.1 broadcast_bitcast_fusion.1
  182.2 43.3 %reduce-scatter.5.cloned.1.call-done = f32[1,256,512]{2,1,0:T(8,128)} async-done(((f32[4,256,512]{2,1,0:T(8,128)}), f32[1,256,512]{2,1,0:T(8,128)}) %reduce-scatter.5.cloned.1.call-update) | async-done | bytes 524304 | tf_op jit(solution)/shard_map/reduce_scatter | solution.py:29
  225.5 1.1 fusion.7
  226.7 31.8 %all-reduce = (f32[512]{0:T(512)S(1)}, f32[512]{0:T(512)S(1)}) all-reduce(f32[512]{0:T(512)S(1)} %broadcast_multiply_fusion.1, f32[512]{0:T(512)S(1)} %fusion.7), channel_id=1, replica_groups=mesh['row'=4,'col'=2,'layer'=4] {'row','layer'}, use_global_device_ids=true, to_apply=%region_2.0 | all-reduce | flops 1024 | bytes 8192 | tf_op jit(solution)/shard_map/psum | solution.py:34
  258.5 1.9 fusion.6
  (6 shorter events, 0.0 us)
Async XLA Ops:
  6.5 28.2 %all-gather.6.cloned.1.call-start = ((), (), s32[]{:S(2)}) async-start(), calls=%async_computation.3 | async-start | bytes 2621440 | tf_op jit(solution)/shard_map/all_gather | solution.py:21
  9.2 83.8 %all-gather.4.cloned.1.call-start = ((), (), s32[]{:S(2)}) async-start(), calls=%async_computation.2 | async-start | bytes 6291456 | tf_op jit(solution)/shard_map/all_gather | solution.py:24
  13.4 134.2 %reduce-scatter.3.cloned.1.call-start = ((), (), s32[]{:S(2)}) async-start(), calls=%async_computation.4 | async-start | bytes 2621440 | tf_op jit(solution)/shard_map/reduce_scatter | solution.py:29
  103.5 67.5 %all-gather.8.cloned.1.call-start = ((), (), s32[]{:S(2)}) async-start(), calls=%async_computation.5 | async-start | bytes 2621440 | tf_op jit(solution)/shard_map/all_gather | solution.py:21
  147.6 78.0 %reduce-scatter.5.cloned.1.call-start = ((), (), s32[]{:S(2)}) async-start(), calls=%async_computation.6 | async-start | bytes 2621440 | tf_op jit(solution)/shard_map/reduce_scatter | solution.py:29
  181.5 0.7 copy-start
Sparse Core Ops, SparseCore 0:
  9.3 25.3 all-gather.5
  36.2 56.7 all-gather.3
  103.7 43.8 reduce-scatter.2
  149.0 21.9 all-gather.7
  181.6 43.8 reduce-scatter.4
where the time goes:
time: 267 us
  waiting for transfers between devices  190 us (71%)
  blocking collectives  31.8 us (12%)
  matrix products  21 us (8%)
  between operations  13.1 us (5%)
  other arithmetic  9.52 us (4%)
    reduce_scatter x2, waiting for transfers between devices, body(): lax.psum_scatter(partial_value, 'layer', scatter_dimension=0, tiled=True)  87.3 us
    all_gather x1, waiting for transfers between devices, body(): lax.all_gather(live_matrix, 'col', axis=3, tiled=True)[:, :, 0, :]  58.3 us
    all_gather x2, waiting for transfers between devices, body(): panel_part = lax.all_gather(current, 'row', axis=1, tiled=True)[0]  44.7 us
    psum x1, blocking collectives, body(): column_total, kept = lax.psum((local_total, local_kept), ('row', 'layer'))  31.8 us
    dot_general x2, matrix products, body(): jnp.einsum('abk,kc->abc', lax.all_gather(live_matrix, 'col', axis=3, tile...  21 us
  transfers between devices with their start and end apart: 5, of which 5 were waited for; matrix products, arithmetic and copies ran while one was open for 2% of the time, Pallas kernels for 0%

commit v1 on v0

v1 whole, which is shorter than its diff:
```python
import functools

import jax
import jax.numpy as jnp
from jax import lax
from jax.experimental import pallas as pl
from jax.experimental.pallas import tpu as pltpu
from jax.sharding import PartitionSpec as P

TILE = 256
MESH = pl.DeviceIdType.MESH
ROW_CHUNKS = 2
COLUMN_CHUNKS = 4
F32 = jnp.float32
BF16 = jnp.bfloat16


def slab_order(layers):
    table = []
    for layer in range(layers):
        up = list(range(layers - 1, layer, -1))
        down = list(range(layer))
        first, second = (up, down) if len(up) >= len(down) else (down, up)
        order = []
        for i in range(len(first)):
            order.append(first[i])
            if i < len(second):
                order.append(second[i])
        table.append(order + [layer])
    return table


def split(value):
    high = value.astype(BF16)
    return high, (value - high.astype(F32)).astype(BF16)


def kernel(
    sizes, mp, pp, op, a_ref, x_ref, sq_ref, tot_ref,
    a_send, a_recv, ah, al, xg, xh, xl, zs1, zr1, zs2, zr2, tz, tr,
    a_ss, a_rs, x_ss, x_fs, x_rs, z1_ss, z1_rs, z2_ss, z2_rs, tz_ss, tz_rs, tr_ss, tr_rs,
):
    n_row, n_col, n_layer = sizes
    slabs, rows, depth = a_ref.shape
    width = x_ref.shape[1]
    rc = rows // ROW_CHUNKS
    wc = width // COLUMN_CHUNKS
    row_tiles, depth_tiles, width_tiles = rows // TILE, depth // TILE, width // TILE
    r, c, l = lax.axis_index("row"), lax.axis_index("col"), lax.axis_index("layer")
    sibling = r + 1 - 2 * lax.rem(r, 2)
    n_x = n_row // 2
    table = slab_order(n_layer)

    def order(s):
        index = l * n_layer + s
        a = jnp.int32(0)
        for i in range(n_layer):
            for j in range(n_layer):
                if table[i][j]:
                    a = jnp.where(index == i * n_layer + j, table[i][j], a)
        return a

    def remote(src, dst, ss, rs, **device):
        return pltpu.make_async_remote_copy(
            src_ref=src, dst_ref=dst, send_sem=ss, recv_sem=rs, device_id=device, device_id_type=MESH
        )

    barrier = pltpu.get_barrier_semaphore()
    for o in range(1, n_col):
        pl.semaphore_signal(barrier, inc=1, device_id={"col": lax.rem(c + o, n_col)}, device_id_type=MESH)
    for o in range(1, n_row):
        pl.semaphore_signal(barrier, inc=1, device_id={"row": lax.rem(r + o, n_row)}, device_id_type=MESH)
    for o in range(1, n_layer):
        pl.semaphore_signal(barrier, inc=1, device_id={"layer": lax.rem(l + o, n_layer)}, device_id_type=MESH)

    def x_copies(step, j):
        own = xg.at[step, r, j]
        yield remote(own, own, x_ss.at[step, j, 0], x_rs.at[step, j, r], row=sibling)
        for o in range(1, n_x):
            yield remote(own, own, x_ss.at[step, j, o], x_rs.at[step, j, r], row=lax.rem(r + 2 * o, n_row))

    def x_forward(step, j, o):
        source = lax.rem(r + n_row - 2 * o, n_row)
        block = xg.at[step, source, j]
        return remote(block, block, x_fs.at[step, j, o - 1], x_rs.at[step, j, source], row=sibling)

    def forward(step, j):
        for o in range(1, n_x):
            copy = x_forward(step, j, o)
            copy.wait_recv()
            copy.start()

    def finish(step, j):
        for o in range(n_x):
            source = lax.rem(sibling + n_row - 2 * o, n_row)
            block = xg.at[step, source, j]
            remote(block, block, x_ss.at[step, j, 0], x_rs.at[step, j, source], row=sibling).wait_recv()
        columns = pl.ds(pl.multiple_of(j * wc, wc), wc)
        for source in range(n_row):
            high, low = split(xg[step, source, j])
            xh[source * rows:(source + 1) * rows, columns] = high
            xl[source * rows:(source + 1) * rows, columns] = low

    def a_copy(o, s, h):
        a = order(s)
        part = pl.ds(pl.multiple_of(h * rc, rc), rc)
        return remote(
            a_send.at[a, part, :], a_recv.at[o - 1, a, part, :], a_ss.at[o - 1, s, h], a_rs.at[o - 1, s, h],
            col=lax.rem(c + o, n_col),
        )

    def keep_a(source, a, part, value):
        columns = pl.ds(pl.multiple_of(source * depth, depth), depth)
        high, low = split(value)
        ah[a, part, columns] = high
        al[a, part, columns] = low

    def product(a, part, columns):
        high = ah[a, part, :]
        right = xh[:, columns]
        total = jnp.dot(high, right, preferred_element_type=F32)
        total += jnp.dot(high, xl[:, columns], preferred_element_type=F32)
        return total + jnp.dot(al[a, part, :], right, preferred_element_type=F32)

    def pass_on(zs, zr, ss, rs, a, s, j):
        upward = a > l
        slot = jnp.where(a == l - 1, n_layer, a)
        target = jnp.where(upward, l + 1, l - 1)

        @pl.when(jnp.where(upward, l, n_layer - 1 - l) > 0)
        def _():
            remote(zs.at[s, j], zr.at[a, j], ss.at[s, j], rs.at[a, j], layer=target).wait_recv()
            zs[s, j] += zr[a, j]

        remote(zs.at[s, j], zr.at[slot, j], ss.at[s, j], rs.at[slot, j], layer=target).start()

    def receive_own(zs, zr, ss, rs, j):
        last = n_layer - 1

        @pl.when(l > 0)
        def _():
            remote(zs.at[last, j], zr.at[l, j], ss.at[0, j], rs.at[l, j], layer=l - 1).wait_recv()
            zs[last, j] += zr[l, j]

        @pl.when(l < last)
        def _():
            remote(zs.at[last, j], zr.at[n_layer, j], ss.at[0, j], rs.at[n_layer, j], layer=l + 1).wait_recv()
            zs[last, j] += zr[n_layer, j]

    def loop(count, body):
        lax.fori_loop(0, count, lambda i, carry: (body(i), carry)[1], 0)

    def mask_x(j):
        tile = (j * wc) // TILE
        for t in range(row_tiles):
            keep = pp[t * width_tiles + tile].astype(F32)
            xg[0, r, j, t * TILE:(t + 1) * TILE, :] = (
                x_ref[t * TILE:(t + 1) * TILE, pl.ds(pl.multiple_of(j * wc, wc), wc)] * keep
            )

    def mask_a(s, h):
        a = order(s)
        part = pl.ds(pl.multiple_of(h * rc, rc), rc)
        for t in range(depth_tiles):
            keep = mp[(a * row_tiles + (h * rc) // TILE) * depth_tiles + t].astype(F32)
            a_send[a, part, t * TILE:(t + 1) * TILE] = a_ref[a, part, t * TILE:(t + 1) * TILE] * keep

    mask_a(0, 0)
    loop(COLUMN_CHUNKS, mask_x)
    pl.semaphore_wait(barrier, n_col + n_row + n_layer - 3)

    def send_a(s, h):
        for o in range(1, n_col):
            a_copy(o, s, h).start()

    def send_x(step):
        def body(j):
            for copy in x_copies(step, j):
                copy.start()
        loop(COLUMN_CHUNKS, body)

    send_a(0, 0)
    send_x(0)

    def start_a(u):
        s, h = u // ROW_CHUNKS, u % ROW_CHUNKS

        @pl.when(u > 0)
        def _():
            mask_a(s, h)
            send_a(s, h)

    loop(n_layer * ROW_CHUNKS, start_a)

    def own_a(u):
        s, h = u // ROW_CHUNKS, u % ROW_CHUNKS
        a = order(s)
        part = pl.ds(pl.multiple_of(h * rc, rc), rc)
        keep_a(c, a, part, a_send[a, part, :])

    loop(n_layer * ROW_CHUNKS, own_a)
    loop(COLUMN_CHUNKS, lambda j: forward(0, j))
    loop(COLUMN_CHUNKS, lambda j: finish(0, j))

    def first(s, h):
        a = order(s)
        part = pl.ds(pl.multiple_of(h * rc, rc), rc)
        for o in range(1, n_col):
            a_copy(o, s, h).wait_recv()
            keep_a(lax.rem(c + n_col - o, n_col), a, part, a_recv[o - 1, a, part, :])
        zs1[s, h] = product(a, part, pl.ds(0, width))
        return a, part

    def first_others(u):
        s, h = u // ROW_CHUNKS, u % ROW_CHUNKS
        a, part = first(s, h)
        pass_on(zs1, zr1, z1_ss, z1_rs, a, s, h)

    loop((n_layer - 1) * ROW_CHUNKS, first_others)

    def first_own(h):
        a, part = first(n_layer - 1, h)
        receive_own(zs1, zr1, z1_ss, z1_rs, h)
        for j in range(COLUMN_CHUNKS):
            xg[1, r, j, part, :] = zs1[n_layer - 1, h, :, j * wc:(j + 1) * wc]

    loop(ROW_CHUNKS, first_own)

    send_x(1)
    whole = pl.ds(0, rows)

    def others(j):
        columns = pl.ds(pl.multiple_of(j * wc, wc), wc)
        finish(1, j)

        def each(s):
            a = order(s)
            zs2[s, j] = product(a, whole, columns)
            pass_on(zs2, zr2, z2_ss, z2_rs, a, s, j)

        loop(n_layer - 1, each)

    def own(j):
        columns = pl.ds(pl.multiple_of(j * wc, wc), wc)
        zs2[n_layer - 1, j] = product(l, whole, columns)
        receive_own(zs2, zr2, z2_ss, z2_rs, j)
        tile = (j * wc) // TILE
        total = jnp.zeros((1, wc), F32)
        kept = jnp.zeros((1, wc), F32)
        for t in range(row_tiles):
            keep = op[t * width_tiles + tile].astype(F32)
            value = zs2[n_layer - 1, j, t * TILE:(t + 1) * TILE, :]
            squared = value * value * keep
            sq_ref[t * TILE:(t + 1) * TILE, columns] = squared
            total += jnp.sum(squared, axis=0, keepdims=True)
            kept += keep * TILE
        tz[l, 0:1, columns] = total
        tz[l, 1:2, columns] = kept

    tz[l] = jnp.zeros_like(tz[l])
    forward(1, 0)

    def second(j):
        @pl.when(j < COLUMN_CHUNKS)
        def _():
            others(j)

        @pl.when(j < COLUMN_CHUNKS - 1)
        def _():
            forward(1, j + 1)

        @pl.when(j > 0)
        def _():
            own(j - 1)

    loop(COLUMN_CHUNKS + 1, second)

    def tz_copy(o):
        return remote(tz.at[l], tz.at[l], tz_ss.at[o - 1], tz_rs.at[o - 1], layer=lax.rem(l + o, n_layer))

    def tr_copy(o):
        return remote(tr.at[r], tr.at[r], tr_ss.at[o - 1], tr_rs.at[o - 1], row=lax.rem(r + o, n_row))

    for o in range(1, n_layer):
        tz_copy(o).start()
    for o in range(1, n_layer):
        source = lax.rem(l + n_layer - o, n_layer)
        remote(tz.at[l], tz.at[source], tz_ss.at[o - 1], tz_rs.at[o - 1], layer=source).wait_recv()
    tr[r] = sum(tz[i] for i in range(n_layer))
    for o in range(1, n_row):
        tr_copy(o).start()
    for o in range(1, n_row):
        source = lax.rem(r + n_row - o, n_row)
        remote(tr.at[r], tr.at[source], tr_ss.at[o - 1], tr_rs.at[o - 1], row=source).wait_recv()
    tot_ref[...] = sum(tr[i] for i in range(n_row))

    def a_left(u):
        s, h = u // ROW_CHUNKS, u % ROW_CHUNKS
        for o in range(1, n_col):
            a_copy(o, s, h).wait_send()

    loop(n_layer * ROW_CHUNKS, a_left)

    def z1_left(u):
        s, h = u // ROW_CHUNKS, u % ROW_CHUNKS
        block = zs1.at[s, h]
        remote(block, block, z1_ss.at[s, h], z1_rs.at[0, h], layer=lax.rem(l + 1, n_layer)).wait_send()

    loop((n_layer - 1) * ROW_CHUNKS, z1_left)

    def chunk_left(j):
        for step in range(2):
            for copy in x_copies(step, j):
                copy.wait_send()
            for o in range(1, n_x):
                x_forward(step, j, o).wait_send()
        for s in range(n_layer - 1):
            block = zs2.at[s, j]
            remote(block, block, z2_ss.at[s, j], z2_rs.at[0, j], layer=lax.rem(l + 1, n_layer)).wait_send()

    loop(COLUMN_CHUNKS, chunk_left)
    for o in range(1, n_layer):
        tz_copy(o).wait_send()
    for o in range(1, n_row):
        tr_copy(o).wait_send()


def body(sizes, matrix_values, matrix_pattern, panel, panel_pattern, out_pattern):
    n_row, n_col, n_layer = sizes
    slabs, rows, _, depth = matrix_values.shape
    width = panel.shape[2]
    inner = depth * n_col
    rc, wc = rows // ROW_CHUNKS, width // COLUMN_CHUNKS
    n_x = n_row // 2
    dma = pltpu.SemaphoreType.DMA
    squared, totals = pl.pallas_call(
        functools.partial(kernel, sizes),
        out_shape=(
            jax.ShapeDtypeStruct((rows, width), F32),
            jax.ShapeDtypeStruct((8, width), F32),
        ),
        in_specs=[pl.BlockSpec(memory_space=pltpu.SMEM)] * 3 + [pl.BlockSpec(memory_space=pltpu.VMEM)] * 2,
        out_specs=(pl.BlockSpec(memory_space=pltpu.VMEM),) * 2,
        scratch_shapes=[
            pltpu.VMEM((slabs, rows, depth), F32),
            pltpu.VMEM((n_col - 1, slabs, rows, depth), F32),
            pltpu.VMEM((slabs, rows, inner), BF16),
            pltpu.VMEM((slabs, rows, inner), BF16),
            pltpu.VMEM((2, n_row, COLUMN_CHUNKS, rows, wc), F32),
            pltpu.VMEM((inner, width), BF16),
            pltpu.VMEM((inner, width), BF16),
            pltpu.VMEM((n_layer, ROW_CHUNKS, rc, width), F32),
            pltpu.VMEM((n_layer + 1, ROW_CHUNKS, rc, width), F32),
            pltpu.VMEM((n_layer, COLUMN_CHUNKS, rows, wc), F32),
            pltpu.VMEM((n_layer + 1, COLUMN_CHUNKS, rows, wc), F32),
            pltpu.VMEM((n_layer, 8, width), F32),
            pltpu.VMEM((n_row, 8, width), F32),
            dma((n_col - 1, n_layer, ROW_CHUNKS)),
            dma((n_col - 1, n_layer, ROW_CHUNKS)),
            dma((2, COLUMN_CHUNKS, n_x)),
            dma((2, COLUMN_CHUNKS, n_x)),
            dma((2, COLUMN_CHUNKS, n_row)),
            dma((n_layer, ROW_CHUNKS)),
            dma((n_layer + 1, ROW_CHUNKS)),
            dma((n_layer, COLUMN_CHUNKS)),
            dma((n_layer + 1, COLUMN_CHUNKS)),
            dma((n_layer - 1,)),
            dma((n_layer - 1,)),
            dma((n_row - 1,)),
            dma((n_row - 1,)),
        ],
        compiler_params=pltpu.CompilerParams(
            collective_id=0, has_side_effects=True, vmem_limit_bytes=56 * 1024 * 1024
        ),
        name="walk",
    )(
        matrix_pattern.reshape(-1),
        panel_pattern.reshape(-1),
        out_pattern.reshape(-1),
        matrix_values.reshape(slabs, rows, depth),
        panel.reshape(rows, width),
    )
    return (squared * (totals[1] / totals[0])[None, :])[None]


def solution(mesh):
    placed = (
        P(None, "row", "layer", "col"),
        P(None, "row", "layer", "col"),
        P("layer", "row", "col"),
        P("layer", "row", "col"),
        P("layer", "row", "col"),
    )
    sizes = (mesh.shape["row"], mesh.shape["col"], mesh.shape["layer"])
    return jax.shard_map(
        functools.partial(body, sizes), mesh=mesh, in_specs=placed, out_specs=P("layer", "row", "col"),
        check_vma=False,
    )
```

time: 267 us -> 117 us (0.44)
  waiting for transfers between devices: 190 us -> 0 us
  Pallas kernels: 0 us -> 110 us
  blocking collectives: 31.8 us -> 0 us
  matrix products: 21 us -> 0 us
  between operations: 13.1 us -> 0.01 us
  other arithmetic: 9.52 us -> 2.7 us
  local copies, waits for them, and re-layouts: 0.96 us -> 4.49 us
    pallas_call x0 -> x1, Pallas kernels: none -> 110 us  [body(): pl.pallas_call(functools.partial(kernel, sizes), out_shape=(jax.ShapeDtyp...]
    all_gather x3 -> x0, waiting for transfers between devices: 103 us -> none  [the longest x1 58.3 us: body(): lax.all_gather(live_matrix, 'col', axis=3, tiled=True)[:, :, 0, :]]
    reduce_scatter x2 -> x0, waiting for transfers between devices: 87.3 us -> none  [body(): lax.psum_scatter(partial_value, 'layer', scatter_dimension=0, tiled=True)]
    psum x1 -> x0, blocking collectives: 31.8 us -> none  [body(): column_total, kept = lax.psum((local_total, local_kept), ('row', 'layer'))]
    dot_general x2 -> x0, matrix products: 21 us -> none  [body(): jnp.einsum('abk,kc->abc', lax.all_gather(live_matrix, 'col', axis=3, tile...]
    mul x3 -> x0, other arithmetic: 7.04 us -> none  [the longest x1 3.22 us: body(): live_matrix = matrix_values * spread(matrix_pattern, (1, 3))]
    unnamed x8 -> x2, local copies, waits for them, and re-layouts: 0.87 us -> 3.89 us
  transfers between devices with their start and end apart: 5 -> 0, of which waited for: 5 -> 0; matrix products, arithmetic and copies ran while one was open for 2% -> 0% of each run, Pallas kernels for 0% -> 0%
where the time goes in v1:
time: 117 us
  Pallas kernels  110 us (94%)
  local copies, waits for them, and re-layouts  4.49 us (4%)
  other arithmetic  2.7 us (2%)
    pallas_call x1, Pallas kernels, body(): pl.pallas_call(functools.partial(kernel, sizes), out_shape=(jax.ShapeDtyp...  110 us
    unnamed x2, local copies, waits for them, and re-layouts  3.89 us

profile of v1, /device:TPU:0, one launch (start us, length us, event | category | flops | bytes accessed | tf_op | source)
XLA Modules:
  0.0 117.0 jit_solution(9602435193270325433)
XLA Ops:
  0.0 0.8 copy.7
  0.8 0.6 reshape.15.mp
  1.4 3.1 %copy.10 = f32[4,256,1,512]{3,1,2,0:T(8,128)} copy(f32[4,256,1,512]{3,2,1,0:T(1,128)} %param.5) | data formatting | bytes 4194304
  4.5 109.8 %walk.1 = (f32[256,512]{1,0:T(8,128)}, f32[8,512]{1,0:T(8,128)}) custom-call(s32[8]{0:T(128)} %reshape.15.mp, s32[2]{0:T(128)} %bitcast.14, s32[2]{0:T(128)} %bitcast.15, f32[4,256,512]{2,1,0:T(8,128)} %bitcast.11, f32[256,512]{1,0:T(8,128)} %bitcast.12), custom_call_target="tpu_custom_call" | custom-call | tf_op jit(solution)/shard_map/walk/pallas_call | solution.py:336
  114.3 0.8 slice_divide_fusion
  115.1 1.9 %multiply_bitcast_fusion = f32[1,256,512]{2,1,0:T(8,128)} fusion(f32[256,512]{1,0:T(8,128)} %get-tuple-element.7, f32[512]{0:T(512)S(1)} %bitcast.13), kind=kLoop, calls=%fused_computation.1 | loop fusion | flops 131072 | bytes 1050624 | tf_op jit(solution)/shard_map/broadcast_in_dim | solution.py:383

commit v2 on v1

--- a/solution.py
+++ b/solution.py
@@ -36,9 +36,9 @@
 
 
 def kernel(
-    sizes, mp, pp, op, a_ref, x_ref, sq_ref, tot_ref,
-    a_send, a_recv, ah, al, xg, xh, xl, zs1, zr1, zs2, zr2, tz, tr,
-    a_ss, a_rs, x_ss, x_fs, x_rs, z1_ss, z1_rs, z2_ss, z2_rs, tz_ss, tz_rs, tr_ss, tr_rs,
+    sizes, mp, pp, op, a_hbm, x_ref, sq_ref, fac_ref,
+    a_ref, a_send, a_recv, ah, al, xg, xh, xl, zs1, zr1, zs2, zr2, tots,
+    a_ls, a_ss, a_rs, x_ss, x_fs, x_rs, z1_ss, z1_rs, z2_ss, z2_rs, t_ss, t_rs,
 ):
     n_row, n_col, n_layer = sizes
     slabs, rows, depth = a_ref.shape
@@ -68,33 +68,42 @@
     barrier = pltpu.get_barrier_semaphore()
     for o in range(1, n_col):
         pl.semaphore_signal(barrier, inc=1, device_id={"col": lax.rem(c + o, n_col)}, device_id_type=MESH)
-    for o in range(1, n_row):
-        pl.semaphore_signal(barrier, inc=1, device_id={"row": lax.rem(r + o, n_row)}, device_id_type=MESH)
-    for o in range(1, n_layer):
-        pl.semaphore_signal(barrier, inc=1, device_id={"layer": lax.rem(l + o, n_layer)}, device_id_type=MESH)
-
-    def x_copies(step, j):
-        own = xg.at[step, r, j]
-        yield remote(own, own, x_ss.at[step, j, 0], x_rs.at[step, j, r], row=sibling)
+    for o in range(1, n_row * n_layer):
+        to_row, to_layer = lax.rem(r + o // n_layer, n_row), lax.rem(l + o % n_layer, n_layer)
+        pl.semaphore_signal(barrier, inc=1, device_id={"row": to_row, "layer": to_layer}, device_id_type=MESH)
+
+    def load_a(s, h):
+        a = order(s)
+        part = pl.ds(pl.multiple_of(h * rc, rc), rc)
+        return pltpu.make_async_copy(a_hbm.at[a, part, 0, :], a_ref.at[a, part, :], a_ls.at[s, h])
+
+    def x_block(step, source, j, h):
+        return xg.at[step, source, j, pl.ds(pl.multiple_of(h * rc, rc), rc), :]
+
+    def x_copies(step, j, h):
+        own = x_block(step, r, j, h)
+        yield remote(own, own, x_ss.at[step, j, h, 0], x_rs.at[step, j, h, r], row=sibling)
         for o in range(1, n_x):
-            yield remote(own, own, x_ss.at[step, j, o], x_rs.at[step, j, r], row=lax.rem(r + 2 * o, n_row))
-
-    def x_forward(step, j, o):
+            yield remote(own, own, x_ss.at[step, j, h, o], x_rs.at[step, j, h, r], row=lax.rem(r + 2 * o, n_row))
+
+    def x_forward(step, j, h, o):
         source = lax.rem(r + n_row - 2 * o, n_row)
-        block = xg.at[step, source, j]
-        return remote(block, block, x_fs.at[step, j, o - 1], x_rs.at[step, j, source], row=sibling)
+        block = x_block(step, source, j, h)
+        return remote(block, block, x_fs.at[step, j, h, o - 1], x_rs.at[step, j, h, source], row=sibling)
 
     def forward(step, j):
-        for o in range(1, n_x):
-            copy = x_forward(step, j, o)
-            copy.wait_recv()
-            copy.start()
+        for h in range(ROW_CHUNKS):
+            for o in range(1, n_x):
+                copy = x_forward(step, j, h, o)
+                copy.wait_recv()
+                copy.start()
 
     def finish(step, j):
-        for o in range(n_x):
-            source = lax.rem(sibling + n_row - 2 * o, n_row)
-            block = xg.at[step, source, j]
-            remote(block, block, x_ss.at[step, j, 0], x_rs.at[step, j, source], row=sibling).wait_recv()
+        for h in range(ROW_CHUNKS):
+            for o in range(n_x):
+                source = lax.rem(sibling + n_row - 2 * o, n_row)
+                block = x_block(step, source, j, h)
+                remote(block, block, x_ss.at[step, j, h, 0], x_rs.at[step, j, h, source], row=sibling).wait_recv()
         columns = pl.ds(pl.multiple_of(j * wc, wc), wc)
         for source in range(n_row):
             high, low = split(xg[step, source, j])
@@ -159,28 +168,29 @@
             )
 
     def mask_a(s, h):
+        load_a(s, h).wait()
         a = order(s)
         part = pl.ds(pl.multiple_of(h * rc, rc), rc)
         for t in range(depth_tiles):
-            keep = mp[(a * row_tiles + (h * rc) // TILE) * depth_tiles + t].astype(F32)
+            keep = mp[(h * rc) // TILE * depth_tiles + t, a].astype(F32)
             a_send[a, part, t * TILE:(t + 1) * TILE] = a_ref[a, part, t * TILE:(t + 1) * TILE] * keep
 
+    loop(n_layer * ROW_CHUNKS, lambda u: load_a(u // ROW_CHUNKS, u % ROW_CHUNKS).start())
+    loop(COLUMN_CHUNKS, mask_x)
     mask_a(0, 0)
-    loop(COLUMN_CHUNKS, mask_x)
-    pl.semaphore_wait(barrier, n_col + n_row + n_layer - 3)
+    pl.semaphore_wait(barrier, n_col - 1 + n_row * n_layer - 1)
 
     def send_a(s, h):
         for o in range(1, n_col):
             a_copy(o, s, h).start()
 
-    def send_x(step):
-        def body(j):
-            for copy in x_copies(step, j):
+    def send_x(step, h):
+        for j in range(COLUMN_CHUNKS):
+            for copy in x_copies(step, j, h):
                 copy.start()
-        loop(COLUMN_CHUNKS, body)
 
     send_a(0, 0)
-    send_x(0)
+    loop(ROW_CHUNKS, lambda h: send_x(0, h))
 
     def start_a(u):
         s, h = u // ROW_CHUNKS, u % ROW_CHUNKS
@@ -223,10 +233,10 @@
         receive_own(zs1, zr1, z1_ss, z1_rs, h)
         for j in range(COLUMN_CHUNKS):
             xg[1, r, j, part, :] = zs1[n_layer - 1, h, :, j * wc:(j + 1) * wc]
+        send_x(1, h)
 
     loop(ROW_CHUNKS, first_own)
 
-    send_x(1)
     whole = pl.ds(0, rows)
 
     def others(j):
@@ -254,10 +264,16 @@
             sq_ref[t * TILE:(t + 1) * TILE, columns] = squared
             total += jnp.sum(squared, axis=0, keepdims=True)
             kept += keep * TILE
-        tz[l, 0:1, columns] = total
-        tz[l, 1:2, columns] = kept
-
-    tz[l] = jnp.zeros_like(tz[l])
+        tots[me, 0:1, columns] = total
+        tots[me, 1:2, columns] = kept
+
+    peers = n_row * n_layer
+    me = r * n_layer + l
+
+    def t_copy(o):
+        to_row, to_layer = lax.rem(r + o // n_layer, n_row), lax.rem(l + o % n_layer, n_layer)
+        return remote(tots.at[me], tots.at[me], t_ss.at[o - 1], t_rs.at[o - 1], row=to_row, layer=to_layer)
+
     forward(1, 0)
 
     def second(j):
@@ -275,24 +291,16 @@
 
     loop(COLUMN_CHUNKS + 1, second)
 
-    def tz_copy(o):
-        return remote(tz.at[l], tz.at[l], tz_ss.at[o - 1], tz_rs.at[o - 1], layer=lax.rem(l + o, n_layer))
-
-    def tr_copy(o):
-        return remote(tr.at[r], tr.at[r], tr_ss.at[o - 1], tr_rs.at[o - 1], row=lax.rem(r + o, n_row))
-
-    for o in range(1, n_layer):
-        tz_copy(o).start()
-    for o in range(1, n_layer):
-        source = lax.rem(l + n_layer - o, n_layer)
-        remote(tz.at[l], tz.at[source], tz_ss.at[o - 1], tz_rs.at[o - 1], layer=source).wait_recv()
-    tr[r] = sum(tz[i] for i in range(n_layer))
-    for o in range(1, n_row):
-        tr_copy(o).start()
-    for o in range(1, n_row):
-        source = lax.rem(r + n_row - o, n_row)
-        remote(tr.at[r], tr.at[source], tr_ss.at[o - 1], tr_rs.at[o - 1], row=source).wait_recv()
-    tot_ref[...] = sum(tr[i] for i in range(n_row))
+    for o in range(1, peers):
+        t_copy(o).start()
+    for o in range(1, peers):
+        source_row, source_layer = lax.rem(r + n_row - o // n_layer, n_row), lax.rem(l + n_layer - o % n_layer, n_layer)
+        landed = tots.at[source_row * n_layer + source_layer]
+        remote(landed, landed, t_ss.at[o - 1], t_rs.at[o - 1], row=source_row, layer=source_layer).wait_recv()
+    everywhere = tots[0]
+    for i in range(1, peers):
+        everywhere += tots[i]
+    fac_ref[...] = everywhere[1:2] / everywhere[0:1]
 
     def a_left(u):
         s, h = u // ROW_CHUNKS, u % ROW_CHUNKS
@@ -310,19 +318,18 @@
 
     def chunk_left(j):
         for step in range(2):
-            for copy in x_copies(step, j):
-                copy.wait_send()
-            for o in range(1, n_x):
-                x_forward(step, j, o).wait_send()
+            for h in range(ROW_CHUNKS):
+                for copy in x_copies(step, j, h):
+                    copy.wait_send()
+                for o in range(1, n_x):
+                    x_forward(step, j, h, o).wait_send()
         for s in range(n_layer - 1):
             block = zs2.at[s, j]
             remote(block, block, z2_ss.at[s, j], z2_rs.at[0, j], layer=lax.rem(l + 1, n_layer)).wait_send()
 
     loop(COLUMN_CHUNKS, chunk_left)
-    for o in range(1, n_layer):
-        tz_copy(o).wait_send()
-    for o in range(1, n_row):
-        tr_copy(o).wait_send()
+    for o in range(1, peers):
+        t_copy(o).wait_send()
 
 
 def body(sizes, matrix_values, matrix_pattern, panel, panel_pattern, out_pattern):
@@ -333,15 +340,17 @@
     rc, wc = rows // ROW_CHUNKS, width // COLUMN_CHUNKS
     n_x = n_row // 2
     dma = pltpu.SemaphoreType.DMA
-    squared, totals = pl.pallas_call(
+    squared, factor = pl.pallas_call(
         functools.partial(kernel, sizes),
         out_shape=(
             jax.ShapeDtypeStruct((rows, width), F32),
-            jax.ShapeDtypeStruct((8, width), F32),
+            jax.ShapeDtypeStruct((1, width), F32),
         ),
-        in_specs=[pl.BlockSpec(memory_space=pltpu.SMEM)] * 3 + [pl.BlockSpec(memory_space=pltpu.VMEM)] * 2,
+        in_specs=[pl.BlockSpec(memory_space=pltpu.SMEM)] * 3
+        + [pl.BlockSpec(memory_space=pl.ANY), pl.BlockSpec(memory_space=pltpu.VMEM)],
         out_specs=(pl.BlockSpec(memory_space=pltpu.VMEM),) * 2,
         scratch_shapes=[
+            pltpu.VMEM((slabs, rows, depth), F32),
             pltpu.VMEM((slabs, rows, depth), F32),
             pltpu.VMEM((n_col - 1, slabs, rows, depth), F32),
             pltpu.VMEM((slabs, rows, inner), BF16),
@@ -353,34 +362,32 @@
             pltpu.VMEM((n_layer + 1, ROW_CHUNKS, rc, width), F32),
             pltpu.VMEM((n_layer, COLUMN_CHUNKS, rows, wc), F32),
             pltpu.VMEM((n_layer + 1, COLUMN_CHUNKS, rows, wc), F32),
-            pltpu.VMEM((n_layer, 8, width), F32),
-            pltpu.VMEM((n_row, 8, width), F32),
+            pltpu.VMEM((n_row * n_layer, 2, width), F32),
+            dma((n_layer, ROW_CHUNKS)),
             dma((n_col - 1, n_layer, ROW_CHUNKS)),
             dma((n_col - 1, n_layer, ROW_CHUNKS)),
-            dma((2, COLUMN_CHUNKS, n_x)),
-            dma((2, COLUMN_CHUNKS, n_x)),
-            dma((2, COLUMN_CHUNKS, n_row)),
+            dma((2, COLUMN_CHUNKS, ROW_CHUNKS, n_x)),
+            dma((2, COLUMN_CHUNKS, ROW_CHUNKS, n_x)),
+            dma((2, COLUMN_CHUNKS, ROW_CHUNKS, n_row)),
             dma((n_layer, ROW_CHUNKS)),
             dma((n_layer + 1, ROW_CHUNKS)),
             dma((n_layer, COLUMN_CHUNKS)),
             dma((n_layer + 1, COLUMN_CHUNKS)),
-            dma((n_layer - 1,)),
-            dma((n_layer - 1,)),
-            dma((n_row - 1,)),
-            dma((n_row - 1,)),
+            dma((n_row * n_layer - 1,)),
+            dma((n_row * n_layer - 1,)),
         ],
         compiler_params=pltpu.CompilerParams(
             collective_id=0, has_side_effects=True, vmem_limit_bytes=56 * 1024 * 1024
         ),
         name="walk",
     )(
-        matrix_pattern.reshape(-1),
+        jnp.transpose(matrix_pattern, (1, 2, 3, 0)).reshape(-1, slabs),
         panel_pattern.reshape(-1),
         out_pattern.reshape(-1),
-        matrix_values.reshape(slabs, rows, depth),
+        matrix_values,
         panel.reshape(rows, width),
     )
-    return (squared * (totals[1] / totals[0])[None, :])[None]
+    return (squared * factor)[None]
 
 
 def solution(mesh):

time: 117 us -> 110 us (0.940)
  local copies, waits for them, and re-layouts: 4.49 us -> 0 us
  Pallas kernels: 110 us -> 108 us
    unnamed x2 -> x0, local copies, waits for them, and re-layouts: 3.89 us -> none
    pallas_call x1, Pallas kernels: 110 us -> 108 us  [body(): pl.pallas_call(functools.partial(kernel, sizes), out_shape=(jax.ShapeDtyp...]
where the time goes in v2:
time: 110 us
  Pallas kernels  108 us (98%)
  other arithmetic  1.91 us (2%)
    pallas_call x1, Pallas kernels, body(): pl.pallas_call(functools.partial(kernel, sizes), out_shape=(jax.ShapeDtyp...  108 us

profile of v2, /device:TPU:0, one launch (start us, length us, event | category | flops | bytes accessed | tf_op | source)
XLA Modules:
  0.0 109.6 jit_solution(13109308155635095682)
XLA Ops:
  0.0 107.7 %walk.1 = (f32[256,512]{1,0:T(8,128)}, f32[1,512]{1,0:T(1,128)}) custom-call(s32[2,4]{1,0:T(2,128)} %bitcast.11, s32[2]{0:T(128)} %bitcast.12, s32[2]{0:T(128)} %bitcast.13, f32[4,256,1,512]{3,2,1,0:T(1,128)} %a_hbm.1, f32[256,512]{1,0:T(8,128)} %bitcast.9), custom_call_target="tpu_custom_call" | custom-call | tf_op jit(solution)/shard_map/walk/pallas_call | solution.py:343
  107.7 1.9 %multiply_bitcast_fusion = f32[1,256,512]{2,1,0:T(8,128)} fusion(f32[256,512]{1,0:T(8,128)} %get-tuple-element.7, f32[512]{0:T(512)} %bitcast.10), kind=kLoop, calls=%fused_computation | loop fusion | flops 131072 | bytes 1050624 | tf_op jit(solution)/shard_map/broadcast_in_dim | solution.py:390

commit v3 on v2

--- a/solution.py
+++ b/solution.py
@@ -36,9 +36,9 @@
 
 
 def kernel(
-    sizes, mp, pp, op, a_hbm, x_ref, sq_ref, fac_ref,
-    a_ref, a_send, a_recv, ah, al, xg, xh, xl, zs1, zr1, zs2, zr2, tots,
-    a_ls, a_ss, a_rs, x_ss, x_fs, x_rs, z1_ss, z1_rs, z2_ss, z2_rs, t_ss, t_rs,
+    sizes, mp, pp, op, a_hbm, x_hbm, sq_hbm, fac_ref,
+    a_ref, x_ref, sq_ref, a_send, a_recv, ah, al, xg, xh, xl, zs1, zr1, zs2, zr2, tots,
+    x_ls, sq_ss, a_ls, a_ss, a_rs, x_ss, x_fs, x_rs, z1_ss, z1_rs, z2_ss, z2_rs, t_ss, t_rs,
 ):
     n_row, n_col, n_layer = sizes
     slabs, rows, depth = a_ref.shape
@@ -68,9 +68,21 @@
     barrier = pltpu.get_barrier_semaphore()
     for o in range(1, n_col):
         pl.semaphore_signal(barrier, inc=1, device_id={"col": lax.rem(c + o, n_col)}, device_id_type=MESH)
-    for o in range(1, n_row * n_layer):
+    peers = n_row * n_layer
+    me = r * n_layer + l
+    for o in range(1, peers):
         to_row, to_layer = lax.rem(r + o // n_layer, n_row), lax.rem(l + o % n_layer, n_layer)
         pl.semaphore_signal(barrier, inc=1, device_id={"row": to_row, "layer": to_layer}, device_id_type=MESH)
+
+    def t_copy(kind, o):
+        to_row, to_layer = lax.rem(r + o // n_layer, n_row), lax.rem(l + o % n_layer, n_layer)
+        own_row = tots.at[kind, me]
+        return remote(own_row, own_row, t_ss.at[kind, o - 1], t_rs.at[kind, o - 1], row=to_row, layer=to_layer)
+
+    def t_landed(kind, o):
+        source_row, source_layer = lax.rem(r + n_row - o // n_layer, n_row), lax.rem(l + n_layer - o % n_layer, n_layer)
+        landed = tots.at[kind, source_row * n_layer + source_layer]
+        return remote(landed, landed, t_ss.at[kind, o - 1], t_rs.at[kind, o - 1], row=source_row, layer=source_layer)
 
     def load_a(s, h):
         a = order(s)
@@ -176,7 +188,8 @@
             a_send[a, part, t * TILE:(t + 1) * TILE] = a_ref[a, part, t * TILE:(t + 1) * TILE] * keep
 
     loop(n_layer * ROW_CHUNKS, lambda u: load_a(u // ROW_CHUNKS, u % ROW_CHUNKS).start())
-    loop(COLUMN_CHUNKS, mask_x)
+    x_load = pltpu.make_async_copy(x_hbm, x_ref, x_ls)
+    x_load.start()
     mask_a(0, 0)
     pl.semaphore_wait(barrier, n_col - 1 + n_row * n_layer - 1)
 
@@ -190,6 +203,8 @@
                 copy.start()
 
     send_a(0, 0)
+    x_load.wait()
+    loop(COLUMN_CHUNKS, mask_x)
     loop(ROW_CHUNKS, lambda h: send_x(0, h))
 
     def start_a(u):
@@ -209,6 +224,13 @@
         keep_a(c, a, part, a_send[a, part, :])
 
     loop(n_layer * ROW_CHUNKS, own_a)
+    for tile in range(width_tiles):
+        kept = jnp.zeros((1, TILE), F32)
+        for t in range(row_tiles):
+            kept += op[t * width_tiles + tile].astype(F32) * TILE
+        tots[0, me, :, tile * TILE:(tile + 1) * TILE] = kept
+    for o in range(1, peers):
+        t_copy(0, o).start()
     loop(COLUMN_CHUNKS, lambda j: forward(0, j))
     loop(COLUMN_CHUNKS, lambda j: finish(0, j))
 
@@ -250,29 +272,24 @@
 
         loop(n_layer - 1, each)
 
+    def sq_copy(j):
+        columns = pl.ds(pl.multiple_of(j * wc, wc), wc)
+        return pltpu.make_async_copy(sq_ref.at[:, columns], sq_hbm.at[:, columns], sq_ss.at[j])
+
     def own(j):
         columns = pl.ds(pl.multiple_of(j * wc, wc), wc)
         zs2[n_layer - 1, j] = product(l, whole, columns)
         receive_own(zs2, zr2, z2_ss, z2_rs, j)
         tile = (j * wc) // TILE
         total = jnp.zeros((1, wc), F32)
-        kept = jnp.zeros((1, wc), F32)
         for t in range(row_tiles):
             keep = op[t * width_tiles + tile].astype(F32)
             value = zs2[n_layer - 1, j, t * TILE:(t + 1) * TILE, :]
             squared = value * value * keep
             sq_ref[t * TILE:(t + 1) * TILE, columns] = squared
             total += jnp.sum(squared, axis=0, keepdims=True)
-            kept += keep * TILE
-        tots[me, 0:1, columns] = total
-        tots[me, 1:2, columns] = kept
-
-    peers = n_row * n_layer
-    me = r * n_layer + l
-
-    def t_copy(o):
-        to_row, to_layer = lax.rem(r + o // n_layer, n_row), lax.rem(l + o % n_layer, n_layer)
-        return remote(tots.at[me], tots.at[me], t_ss.at[o - 1], t_rs.at[o - 1], row=to_row, layer=to_layer)
+        tots[1, me, :, columns] = total
+        sq_copy(j).start()
 
     forward(1, 0)
 
@@ -292,15 +309,13 @@
     loop(COLUMN_CHUNKS + 1, second)
 
     for o in range(1, peers):
-        t_copy(o).start()
-    for o in range(1, peers):
-        source_row, source_layer = lax.rem(r + n_row - o // n_layer, n_row), lax.rem(l + n_layer - o % n_layer, n_layer)
-        landed = tots.at[source_row * n_layer + source_layer]
-        remote(landed, landed, t_ss.at[o - 1], t_rs.at[o - 1], row=source_row, layer=source_layer).wait_recv()
-    everywhere = tots[0]
-    for i in range(1, peers):
-        everywhere += tots[i]
-    fac_ref[...] = everywhere[1:2] / everywhere[0:1]
+        t_copy(1, o).start()
+    for o in range(1, peers):
+        t_landed(0, o).wait_recv()
+    counted = sum(tots[0, i] for i in range(peers))
+    for o in range(1, peers):
+        t_landed(1, o).wait_recv()
+    fac_ref[...] = counted / sum(tots[1, i] for i in range(peers))
 
     def a_left(u):
         s, h = u // ROW_CHUNKS, u % ROW_CHUNKS
@@ -328,8 +343,10 @@
             remote(block, block, z2_ss.at[s, j], z2_rs.at[0, j], layer=lax.rem(l + 1, n_layer)).wait_send()
 
     loop(COLUMN_CHUNKS, chunk_left)
-    for o in range(1, peers):
-        t_copy(o).wait_send()
+    loop(COLUMN_CHUNKS, lambda j: sq_copy(j).wait())
+    for o in range(1, peers):
+        t_copy(0, o).wait_send()
+        t_copy(1, o).wait_send()
 
 
 def body(sizes, matrix_values, matrix_pattern, panel, panel_pattern, out_pattern):
@@ -347,10 +364,12 @@
             jax.ShapeDtypeStruct((1, width), F32),
         ),
         in_specs=[pl.BlockSpec(memory_space=pltpu.SMEM)] * 3
-        + [pl.BlockSpec(memory_space=pl.ANY), pl.BlockSpec(memory_space=pltpu.VMEM)],
-        out_specs=(pl.BlockSpec(memory_space=pltpu.VMEM),) * 2,
+        + [pl.BlockSpec(memory_space=pl.ANY)] * 2,
+        out_specs=(pl.BlockSpec(memory_space=pl.ANY), pl.BlockSpec(memory_space=pltpu.VMEM)),
         scratch_shapes=[
             pltpu.VMEM((slabs, rows, depth), F32),
+            pltpu.VMEM((rows, width), F32),
+            pltpu.VMEM((rows, width), F32),
             pltpu.VMEM((slabs, rows, depth), F32),
             pltpu.VMEM((n_col - 1, slabs, rows, depth), F32),
             pltpu.VMEM((slabs, rows, inner), BF16),
@@ -362,7 +381,9 @@
             pltpu.VMEM((n_layer + 1, ROW_CHUNKS, rc, width), F32),
             pltpu.VMEM((n_layer, COLUMN_CHUNKS, rows, wc), F32),
             pltpu.VMEM((n_layer + 1, COLUMN_CHUNKS, rows, wc), F32),
-            pltpu.VMEM((n_row * n_layer, 2, width), F32),
+            pltpu.VMEM((2, n_row * n_layer, 1, width), F32),
+            dma,
+            dma((COLUMN_CHUNKS,)),
             dma((n_layer, ROW_CHUNKS)),
             dma((n_col - 1, n_layer, ROW_CHUNKS)),
             dma((n_col - 1, n_layer, ROW_CHUNKS)),
@@ -373,8 +394,8 @@
             dma((n_layer + 1, ROW_CHUNKS)),
             dma((n_layer, COLUMN_CHUNKS)),
             dma((n_layer + 1, COLUMN_CHUNKS)),
-            dma((n_row * n_layer - 1,)),
-            dma((n_row * n_layer - 1,)),
+            dma((2, n_row * n_layer - 1)),
+            dma((2, n_row * n_layer - 1)),
         ],
         compiler_params=pltpu.CompilerParams(
             collective_id=0, has_side_effects=True, vmem_limit_bytes=56 * 1024 * 1024

time: 110 us -> 109 us (level)
  no operation moved by 1% of the time
where the time goes in v3:
time: 109 us
  Pallas kernels  107 us (98%)
  other arithmetic  1.91 us (2%)
    pallas_call x1, Pallas kernels, body(): pl.pallas_call(functools.partial(kernel, sizes), out_shape=(jax.ShapeDtyp...  107 us

profile of v3, /device:TPU:0, one launch (start us, length us, event | category | flops | bytes accessed | tf_op | source)
XLA Modules:
  0.0 109.1 jit_solution(17519167960839588043)
XLA Ops:
  0.0 107.2 %walk.1 = (f32[256,512]{1,0:T(8,128)}, f32[1,512]{1,0:T(1,128)}) custom-call(s32[2,4]{1,0:T(2,128)} %bitcast.11, s32[2]{0:T(128)} %bitcast.12, s32[2]{0:T(128)} %bitcast.13, f32[4,256,1,512]{3,2,1,0:T(1,128)} %a_hbm.1, f32[256,512]{1,0:T(8,128)} %bitcast.9), custom_call_target="tpu_custom_call" | custom-call | tf_op jit(solution)/shard_map/walk/pallas_call | solution.py:360
  107.2 1.9 %multiply_bitcast_fusion = f32[1,256,512]{2,1,0:T(8,128)} fusion(f32[256,512]{1,0:T(8,128)} %get-tuple-element.7, f32[512]{0:T(512)} %bitcast.10), kind=kLoop, calls=%fused_computation | loop fusion | flops 131072 | bytes 1050624 | tf_op jit(solution)/shard_map/broadcast_in_dim | solution.py:411

commit v4 on v3

--- a/solution.py
+++ b/solution.py
@@ -310,12 +310,6 @@
 
     for o in range(1, peers):
         t_copy(1, o).start()
-    for o in range(1, peers):
-        t_landed(0, o).wait_recv()
-    counted = sum(tots[0, i] for i in range(peers))
-    for o in range(1, peers):
-        t_landed(1, o).wait_recv()
-    fac_ref[...] = counted / sum(tots[1, i] for i in range(peers))
 
     def a_left(u):
         s, h = u // ROW_CHUNKS, u % ROW_CHUNKS
@@ -346,6 +340,14 @@
     loop(COLUMN_CHUNKS, lambda j: sq_copy(j).wait())
     for o in range(1, peers):
         t_copy(0, o).wait_send()
+
+    for o in range(1, peers):
+        t_landed(0, o).wait_recv()
+    counted = sum(tots[0, i] for i in range(peers))
+    for o in range(1, peers):
+        t_landed(1, o).wait_recv()
+    fac_ref[...] = counted / sum(tots[1, i] for i in range(peers))
+    for o in range(1, peers):
         t_copy(1, o).wait_send()
 
 

time: 109 us -> 109 us (level)
  no operation moved by 1% of the time
where the time goes in v4:
time: 109 us
  Pallas kernels  107 us (98%)
  other arithmetic  1.91 us (2%)
    pallas_call x1, Pallas kernels, body(): pl.pallas_call(functools.partial(kernel, sizes), out_shape=(jax.ShapeDtyp...  107 us

profile of v4, /device:TPU:0, one launch (start us, length us, event | category | flops | bytes accessed | tf_op | source)
XLA Modules:
  0.0 108.8 jit_solution(16871186775317146922)
XLA Ops:
  0.0 106.9 %walk.1 = (f32[256,512]{1,0:T(8,128)}, f32[1,512]{1,0:T(1,128)}) custom-call(s32[2,4]{1,0:T(2,128)} %bitcast.11, s32[2]{0:T(128)} %bitcast.12, s32[2]{0:T(128)} %bitcast.13, f32[4,256,1,512]{3,2,1,0:T(1,128)} %a_hbm.1, f32[256,512]{1,0:T(8,128)} %bitcast.9), custom_call_target="tpu_custom_call" | custom-call | tf_op jit(solution)/shard_map/walk/pallas_call | solution.py:362
  106.9 1.9 %multiply_bitcast_fusion = f32[1,256,512]{2,1,0:T(8,128)} fusion(f32[256,512]{1,0:T(8,128)} %get-tuple-element.7, f32[512]{0:T(512)} %bitcast.10), kind=kLoop, calls=%fused_computation | loop fusion | flops 131072 | bytes 1050624 | tf_op jit(solution)/shard_map/broadcast_in_dim | solution.py:413
